TPU v7x, 32 devices: a whole 2x2x4 slice. The times are simulated.
32 devices in a mesh: dp: 8 (over y, x, core), expert: 4 (over z).
Axes of the slice: x: 2, y: 2, z: 4, core: 2. Of those that a mesh axis runs over, the one named last changes fastest.
Arguments:
- tokens: bfloat16 [4096, 1024], P(('dp', 'expert')), may hold values from -6 to 6
- first_gain: bfloat16 [1024], P(('dp', 'expert')), may hold values from 0.5 to 1.5
- w_qkv: bfloat16 [1024, 3072], P(('dp', 'expert')), may hold values from -0.1875 to 0.1875
- w_out: bfloat16 [1024, 1024], P(('dp', 'expert')), may hold values from -1 to 1
- second_gain: bfloat16 [1024], P(('dp', 'expert')), may hold values from 0.5 to 1.5
- w_mix: bfloat16 [1024, 2], P(('dp', 'expert')), may hold values from -0.1875 to 0.1875
- w_up: bfloat16 [1024, 4096], P(('dp', 'expert')), may hold values from -0.1875 to 0.1875
- w_down: bfloat16 [4096, 1024], P(('dp', 'expert')), may hold values from -0.1875 to 0.1875
- expert_up: bfloat16 [4, 1024, 4096], P('expert', 'dp'), may hold values from -0.1875 to 0.1875
- expert_down: bfloat16 [4, 4096, 1024], P('expert', 'dp'), may hold values from -0.1875 to 0.1875
- expert_ids: int32 [4096, 1], P(('dp', 'expert')), may hold values from 0 to 3; in each aligned block of 128 rows (0 to 127, 128 to 255, ...) at most 40 rows name the same one
- doc_lengths: int32 [8, 2], P('dp'), may hold values from 64 to 448, as said below
- out_grad: bfloat16 [4096, 1024], P(('dp', 'expert')), may hold values from -6 to 6
Outputs:
- output: bfloat16 [4096, 1024], P(('dp', 'expert'))
- tokens_grad: bfloat16 [4096, 1024], P(('dp', 'expert'))
- first_gain_grad: float32 [1024], P(('dp', 'expert'))
- w_qkv_grad: float32 [1024, 3072], P(('dp', 'expert'))
- w_out_grad: float32 [1024, 1024], P(('dp', 'expert'))
- second_gain_grad: float32 [1024], P(('dp', 'expert'))
- w_mix_grad: float32 [1024, 2], P(('dp', 'expert'))
- w_up_grad: float32 [1024, 4096], P(('dp', 'expert'))
- w_down_grad: float32 [4096, 1024], P(('dp', 'expert'))
- expert_up_grad: float32 [4, 1024, 4096], P('expert', 'dp')
- expert_down_grad: float32 [4, 4096, 1024], P('expert', 'dp')
Inputs may be any that keep to these rules, and one draw needn't show every extreme that they name: `expert_ids`: in each device's 128 rows no expert is chosen more than 40 times, a bound that some block reaches in some of them. `doc_lengths`: the two lengths of a group sum to 512; the longer is exactly 448 and stands first or second.
All inputs are finite; a program needn't handle non-finite values.
Results may differ from a plain program's by a relative error of at most 0.015.
Values may be sent and summed in bfloat16 or wider, within the bound.
No kernel may reach another device: no remote copies, remote signals or barrier semaphores. Data moves between devices by JAX's collectives and lax.ppermute only.
A program may use at most 256 MiB of HBM per device.

v0:
```python
import jax
import jax.numpy as jnp
from jax import lax
from jax.sharding import PartitionSpec as P

HEAD_DIM = 64


EPSILON = 1e-05
SCORE_SCALE = 0.125
MASK_VALUE = -1e30


def norm_rows(values, gain_vec):
    row_mean = jnp.mean(values, axis=-1, keepdims=True)
    centred = values - row_mean
    spread = jnp.mean(centred * centred, axis=-1, keepdims=True)
    return centred * lax.rsqrt(spread + EPSILON) * gain_vec


def smooth(values):
    return jax.nn.gelu(values, approximate=True)


def key_blocks(gathered):
    key_total = gathered.shape[0]
    block_size = min(512, key_total)
    block_count = key_total // block_size
    blocks = gathered.reshape(block_count, block_size, gathered.shape[1])
    starts = jnp.arange(block_count, dtype=jnp.int32) * block_size
    return (blocks, starts)


def block_scores(query_heads, kv_block, block_start, query_pos, doc_split):
    block_size = kv_block.shape[0]
    head_count = query_heads.shape[1]
    feat_width = head_count * HEAD_DIM
    key_heads = kv_block[:, :feat_width].reshape(block_size, head_count, HEAD_DIM)
    value_heads = kv_block[:, feat_width:].reshape(block_size, head_count, HEAD_DIM)
    scores = (
        jnp.einsum("qhd,khd->hqk", query_heads, key_heads, preferred_element_type=jnp.float32)
        * SCORE_SCALE
    )
    key_pos = block_start + jnp.arange(block_size, dtype=jnp.int32)
    allowed = (query_pos[:, None] >= key_pos[None, :]) & (
        (query_pos[:, None] >= doc_split) == (key_pos[None, :] >= doc_split)
    )
    return (scores, allowed[None], key_heads, value_heads)


def attend(query_heads, gathered, query_pos, doc_split):
    row_count, head_count = (query_heads.shape[0], query_heads.shape[1])
    blocks, starts = key_blocks(gathered)

    def stat_step(state_pair, block_item):
        running_max, exp_total = state_pair
        scores, allowed, key_heads, value_heads = block_scores(
            query_heads, block_item[0], block_item[1], query_pos, doc_split
        )
        masked = jnp.where(allowed, scores, MASK_VALUE)
        new_max = jnp.maximum(running_max, jnp.max(masked, axis=-1))
        weights = jnp.where(allowed, jnp.exp(masked - new_max[..., None]), 0.0)
        exp_total = exp_total * jnp.exp(running_max - new_max) + jnp.sum(weights, axis=-1)
        return ((new_max, exp_total), None)

    start_pair = (
        jnp.full((head_count, row_count), MASK_VALUE, jnp.float32),
        jnp.zeros((head_count, row_count), jnp.float32),
    )
    (running_max, exp_total), unused = lax.scan(stat_step, start_pair, (blocks, starts))
    log_total = running_max + jnp.log(exp_total)

    def value_step(accumulated, block_item):
        scores, allowed, key_heads, value_heads = block_scores(
            query_heads, block_item[0], block_item[1], query_pos, doc_split
        )
        weights_low = jnp.where(allowed, jnp.exp(scores - log_total[..., None]), 0.0).astype(
            jnp.bfloat16
        )
        return (
            accumulated
            + jnp.einsum(
                "hqk,khd->qhd", weights_low, value_heads, preferred_element_type=jnp.float32
            ),
            None,
        )

    accumulated, unused = lax.scan(
        value_step, jnp.zeros((row_count, head_count, HEAD_DIM), jnp.float32), (blocks, starts)
    )
    return (accumulated, log_total)


def delta_of(query_heads, gathered, query_pos, doc_split, log_total, grad_heads):
    row_count, head_count = (query_heads.shape[0], query_heads.shape[1])
    blocks, starts = key_blocks(gathered)

    def delta_step(delta_sum, block_item):
        scores, allowed, key_heads, value_heads = block_scores(
            query_heads, block_item[0], block_item[1], query_pos, doc_split
        )
        weights = jnp.where(allowed, jnp.exp(scores - log_total[..., None]), 0.0)
        dweights = jnp.einsum(
            "qhd,khd->hqk", grad_heads, value_heads, preferred_element_type=jnp.float32
        )
        return (delta_sum + jnp.sum(weights * dweights, axis=-1), None)

    delta_sum, unused = lax.scan(
        delta_step, jnp.zeros((head_count, row_count), jnp.float32), (blocks, starts)
    )
    return delta_sum


def attend_back(query_heads, gathered, query_pos, doc_split, log_total, grad_heads, delta_sum):
    row_count, head_count = (query_heads.shape[0], query_heads.shape[1])
    blocks, starts = key_blocks(gathered)

    def grad_step(dquery, block_item):
        scores, allowed, key_heads, value_heads = block_scores(
            query_heads, block_item[0], block_item[1], query_pos, doc_split
        )
        weights = jnp.where(allowed, jnp.exp(scores - log_total[..., None]), 0.0)
        dweights = jnp.einsum(
            "qhd,khd->hqk", grad_heads, value_heads, preferred_element_type=jnp.float32
        )
        dscores = (weights * (dweights - delta_sum[..., None])).astype(jnp.bfloat16)
        dquery = dquery + jnp.einsum(
            "hqk,khd->qhd", dscores, key_heads, preferred_element_type=jnp.float32
        )
        return (dquery, None)

    dquery, pairs = lax.scan(
        grad_step, jnp.zeros((row_count, head_count, HEAD_DIM), jnp.float32), (blocks, starts)
    )
    return (dquery * SCORE_SCALE, None)


def own_key_grads(own_kv, key_pos, group_query, group_grad, group_log, group_delta, doc_split):
    query_total = group_query.shape[0]
    row_count = own_kv.shape[0]
    head_count = group_log.shape[1]
    feat_width = head_count * HEAD_DIM
    key_heads = own_kv[:, :feat_width].reshape(row_count, head_count, HEAD_DIM)
    value_heads = own_kv[:, feat_width:].reshape(row_count, head_count, HEAD_DIM)
    block_size = min(512, query_total)
    block_count = query_total // block_size
    query_blocks = group_query.reshape(block_count, block_size, head_count, HEAD_DIM)
    grad_blocks = group_grad.reshape(block_count, block_size, head_count, HEAD_DIM)
    log_blocks = group_log.reshape(block_count, block_size, head_count)
    delta_blocks = group_delta.reshape(block_count, block_size, head_count)
    starts = jnp.arange(block_count, dtype=jnp.int32) * block_size

    def key_step(carried, block_item):
        dkeys, dvalues = carried
        query_block, grad_block, log_block, delta_block, block_start = block_item
        query_pos = block_start + jnp.arange(block_size, dtype=jnp.int32)
        scores = (
            jnp.einsum("qhd,khd->hqk", query_block, key_heads, preferred_element_type=jnp.float32)
            * SCORE_SCALE
        )
        allowed = (query_pos[:, None] >= key_pos[None, :]) & (
            (query_pos[:, None] >= doc_split) == (key_pos[None, :] >= doc_split)
        )
        weights = jnp.where(allowed[None], jnp.exp(scores - log_block.T[..., None]), 0.0)
        dweights = jnp.einsum(
            "qhd,khd->hqk", grad_block, value_heads, preferred_element_type=jnp.float32
        )
        dscores = (weights * (dweights - delta_block.T[..., None])).astype(jnp.bfloat16)
        dkeys = dkeys + jnp.einsum(
            "hqk,qhd->khd", dscores, query_block, preferred_element_type=jnp.float32
        )
        dvalues = dvalues + jnp.einsum(
            "hqk,qhd->khd",
            weights.astype(jnp.bfloat16),
            grad_block,
            preferred_element_type=jnp.float32,
        )
        return ((dkeys, dvalues), None)

    empty = jnp.zeros((row_count, head_count, HEAD_DIM), jnp.float32)
    (dkeys, dvalues), unused = lax.scan(
        key_step, (empty, empty), (query_blocks, grad_blocks, log_blocks, delta_blocks, starts)
    )
    return jnp.concatenate(
        [
            (dkeys * SCORE_SCALE).reshape(row_count, feat_width),
            dvalues.reshape(row_count, feat_width),
        ],
        axis=1,
    )


def shards(
    tokens,
    first_gain,
    w_qkv,
    w_out,
    second_gain,
    w_mix,
    w_up,
    w_down,
    expert_up,
    expert_down,
    expert_ids,
    doc_lengths,
    out_grad,
):
    row_count, feat_width = tokens.shape
    head_count = feat_width // HEAD_DIM
    gain_one, qkv_matrix, out_matrix = (
        lax.all_gather(first_gain, ("dp", "expert"), axis=0, tiled=True),
        lax.all_gather(w_qkv, ("dp", "expert"), axis=0, tiled=True),
        lax.all_gather(w_out, ("dp", "expert"), axis=0, tiled=True),
    )
    gain_two, mix_matrix, up_matrix, down_matrix = (
        lax.all_gather(second_gain, ("dp", "expert"), axis=0, tiled=True),
        lax.all_gather(w_mix, ("dp", "expert"), axis=0, tiled=True),
        lax.all_gather(w_up, ("dp", "expert"), axis=0, tiled=True),
        lax.all_gather(w_down, ("dp", "expert"), axis=0, tiled=True),
    )
    own_up, own_down = (
        lax.all_gather(expert_up, "dp", axis=1, tiled=True),
        lax.all_gather(expert_down, "dp", axis=1, tiled=True),
    )
    own_up = own_up[0]
    own_down = own_down[0]
    inputs = tokens.astype(jnp.float32)
    attn_input = norm_rows(inputs, gain_one.astype(jnp.float32)).astype(jnp.bfloat16)
    qkv = jnp.dot(attn_input, qkv_matrix, preferred_element_type=jnp.float32).astype(jnp.bfloat16)
    query_flat = qkv[:, :feat_width]
    query_heads = query_flat.reshape(row_count, head_count, HEAD_DIM)
    own_kv = qkv[:, feat_width:]
    gathered = lax.all_gather(own_kv, "expert", axis=0, tiled=True)
    doc_split = doc_lengths[0, 0]
    query_pos = lax.axis_index("expert") * row_count + jnp.arange(row_count, dtype=jnp.int32)
    accumulated, log_total = attend(query_heads, gathered, query_pos, doc_split)
    attended = accumulated.reshape(row_count, feat_width).astype(jnp.bfloat16)
    middle = inputs + jnp.dot(attended, out_matrix, preferred_element_type=jnp.float32)
    ffn_input = norm_rows(middle, gain_two.astype(jnp.float32)).astype(jnp.bfloat16)
    coeffs = jax.nn.softmax(
        jnp.dot(ffn_input, mix_matrix, preferred_element_type=jnp.float32), axis=-1
    )
    dense_pre = jnp.dot(ffn_input, up_matrix, preferred_element_type=jnp.float32)
    dense_act = smooth(dense_pre).astype(jnp.bfloat16)
    dense_out = jnp.dot(dense_act, down_matrix, preferred_element_type=jnp.float32)
    expert_count = lax.axis_size("expert")
    capacity = max(2, 5 * row_count // (4 * expert_count))
    expert_choice = expert_ids[:, 0]
    onehot = (expert_choice[:, None] == jnp.arange(expert_count, dtype=jnp.int32)[None, :]).astype(
        jnp.int32
    )
    slot_rank = jnp.sum((jnp.cumsum(onehot, axis=0) - 1) * onehot, axis=1)
    slot_index = expert_choice * capacity + slot_rank
    outgoing = (
        jnp.zeros((expert_count * capacity, feat_width), jnp.bfloat16).at[slot_index].set(ffn_input)
    )
    outgoing = outgoing.reshape(expert_count, capacity, feat_width)
    incoming = lax.all_to_all(outgoing, "expert", split_axis=0, concat_axis=0, tiled=True)
    expert_pre = jnp.einsum("sid,df->sif", incoming, own_up, preferred_element_type=jnp.float32)
    result = jnp.einsum(
        "sif,fd->sid",
        smooth(expert_pre).astype(jnp.bfloat16),
        own_down,
        preferred_element_type=jnp.float32,
    ).astype(jnp.bfloat16)
    returned_rows = lax.all_to_all(result, "expert", split_axis=0, concat_axis=0, tiled=True)
    returned, received, expert_pre = (returned_rows, incoming, expert_pre)
    expert_rows = returned.reshape(expert_count * capacity, feat_width)[slot_index].astype(
        jnp.float32
    )
    output = middle + coeffs[:, 0:1] * dense_out + coeffs[:, 1:2] * expert_rows
    gain_one, qkv_matrix, out_matrix = (
        lax.all_gather(first_gain, ("dp", "expert"), axis=0, tiled=True),
        lax.all_gather(w_qkv, ("dp", "expert"), axis=0, tiled=True),
        lax.all_gather(w_out, ("dp", "expert"), axis=0, tiled=True),
    )
    gain_two, mix_matrix, up_matrix, down_matrix = (
        lax.all_gather(second_gain, ("dp", "expert"), axis=0, tiled=True),
        lax.all_gather(w_mix, ("dp", "expert"), axis=0, tiled=True),
        lax.all_gather(w_up, ("dp", "expert"), axis=0, tiled=True),
        lax.all_gather(w_down, ("dp", "expert"), axis=0, tiled=True),
    )
    grad_output = out_grad.astype(jnp.float32)
    dcoeffs = jnp.stack(
        [jnp.sum(grad_output * dense_out, axis=1), jnp.sum(grad_output * expert_rows, axis=1)],
        axis=1,
    )
    dlogits = (coeffs * (dcoeffs - jnp.sum(coeffs * dcoeffs, axis=1, keepdims=True))).astype(
        jnp.bfloat16
    )
    ddense = (coeffs[:, 0:1] * grad_output).astype(jnp.bfloat16)
    dexpert = (coeffs[:, 1:2] * grad_output).astype(jnp.bfloat16)
    back_rows = (
        jnp.zeros((expert_count * capacity, feat_width), jnp.bfloat16).at[slot_index].set(dexpert)
    )
    arriving = lax.all_to_all(
        back_rows.reshape(expert_count, capacity, feat_width),
        "expert",
        split_axis=0,
        concat_axis=0,
        tiled=True,
    )
    flat_in = received.reshape(-1, feat_width)
    flat_pre = expert_pre.reshape(flat_in.shape[0], -1)
    flat_grad = arriving.reshape(-1, feat_width)
    grad_expert_down = jnp.einsum(
        "rf,rd->fd",
        smooth(flat_pre).astype(jnp.bfloat16),
        flat_grad,
        preferred_element_type=jnp.float32,
    )
    dexpert_act = jnp.einsum("rd,fd->rf", flat_grad, own_down, preferred_element_type=jnp.float32)
    dexpert_pre = jax.vjp(smooth, flat_pre)[1](dexpert_act)[0].astype(jnp.bfloat16)
    grad_expert_up = jnp.einsum(
        "rd,rf->df", flat_in, dexpert_pre, preferred_element_type=jnp.float32
    )
    dexpert_in = jnp.einsum(
        "rf,df->rd", dexpert_pre, own_up, preferred_element_type=jnp.float32
    ).astype(jnp.bfloat16)
    sent_back = lax.all_to_all(
        dexpert_in.reshape(expert_count, capacity, feat_width),
        "expert",
        split_axis=0,
        concat_axis=0,
        tiled=True,
    )
    expert_part = sent_back.reshape(expert_count * capacity, feat_width)[slot_index].astype(
        jnp.float32
    )
    expert_up_grad, expert_down_grad = (
        lax.psum_scatter(
            grad_expert_up[None].astype(jnp.bfloat16), "dp", scatter_dimension=1, tiled=True
        ).astype(jnp.float32),
        lax.psum_scatter(
            grad_expert_down[None].astype(jnp.bfloat16), "dp", scatter_dimension=1, tiled=True
        ).astype(jnp.float32),
    )
    grad_down = jnp.einsum("rf,rd->fd", dense_act, ddense, preferred_element_type=jnp.float32)
    ddense_act = jnp.einsum("rd,fd->rf", ddense, down_matrix, preferred_element_type=jnp.float32)
    ddense_pre = jax.vjp(smooth, dense_pre)[1](ddense_act)[0].astype(jnp.bfloat16)
    grad_up = jnp.einsum("rd,rf->df", ffn_input, ddense_pre, preferred_element_type=jnp.float32)
    grad_mix = jnp.einsum("rd,rc->dc", ffn_input, dlogits, preferred_element_type=jnp.float32)
    dffn = jnp.einsum("rf,df->rd", ddense_pre, up_matrix, preferred_element_type=jnp.float32)
    dffn = (
        dffn
        + jnp.einsum("rc,dc->rd", dlogits, mix_matrix, preferred_element_type=jnp.float32)
        + expert_part
    )
    dmiddle_part, grad_gain_two = jax.vjp(norm_rows, middle, gain_two.astype(jnp.float32))[1](dffn)
    dmiddle = grad_output + dmiddle_part
    second_gain_grad, w_mix_grad, w_up_grad, w_down_grad = (
        lax.psum_scatter(grad_gain_two, ("dp", "expert"), scatter_dimension=0, tiled=True),
        lax.psum_scatter(grad_mix, ("dp", "expert"), scatter_dimension=0, tiled=True),
        lax.psum_scatter(grad_up, ("dp", "expert"), scatter_dimension=0, tiled=True),
        lax.psum_scatter(grad_down, ("dp", "expert"), scatter_dimension=0, tiled=True),
    )
    dmid_low = dmiddle.astype(jnp.bfloat16)
    grad_out_matrix = jnp.einsum(
        "rd,re->de", attended, dmid_low, preferred_element_type=jnp.float32
    )
    dattended = jnp.einsum(
        "re,de->rd", dmid_low, out_matrix, preferred_element_type=jnp.float32
    ).astype(jnp.bfloat16)
    grad_heads = dattended.reshape(row_count, head_count, HEAD_DIM)
    delta_sum = delta_of(query_heads, gathered, query_pos, doc_split, log_total, grad_heads)
    dquery, unused = attend_back(
        query_heads, gathered, query_pos, doc_split, log_total, grad_heads, delta_sum
    )
    group_query, group_grad = (
        lax.all_gather(query_flat, "expert", axis=0, tiled=True),
        lax.all_gather(dattended, "expert", axis=0, tiled=True),
    )
    group_log, group_delta = (
        lax.all_gather(log_total.T, "expert", axis=0, tiled=True),
        lax.all_gather(delta_sum.T, "expert", axis=0, tiled=True),
    )
    query_total = group_query.shape[0]
    own_pairs = own_key_grads(
        own_kv,
        query_pos,
        group_query.reshape(query_total, head_count, HEAD_DIM),
        group_grad.reshape(query_total, head_count, HEAD_DIM),
        group_log,
        group_delta,
        doc_split,
    )
    dpair = own_pairs.astype(jnp.bfloat16)
    dqkv = jnp.concatenate(
        [dquery.reshape(row_count, feat_width).astype(jnp.bfloat16), dpair], axis=1
    )
    grad_qkv = jnp.einsum("rd,re->de", attn_input, dqkv, preferred_element_type=jnp.float32)
    dattn_input = jnp.einsum("re,de->rd", dqkv, qkv_matrix, preferred_element_type=jnp.float32)
    dinput_part, grad_gain_one = jax.vjp(norm_rows, inputs, gain_one.astype(jnp.float32))[1](
        dattn_input
    )
    tokens_grad = (dmiddle + dinput_part).astype(jnp.bfloat16)
    first_gain_grad, w_qkv_grad, w_out_grad = (
        lax.psum_scatter(grad_gain_one, ("dp", "expert"), scatter_dimension=0, tiled=True),
        lax.psum_scatter(grad_qkv, ("dp", "expert"), scatter_dimension=0, tiled=True),
        lax.psum_scatter(grad_out_matrix, ("dp", "expert"), scatter_dimension=0, tiled=True),
    )
    return (
        output.astype(jnp.bfloat16),
        tokens_grad,
        first_gain_grad,
        w_qkv_grad,
        w_out_grad,
        second_gain_grad,
        w_mix_grad,
        w_up_grad,
        w_down_grad,
        expert_up_grad,
        expert_down_grad,
    )


def solution(mesh):
    placed = (
        P(("dp", "expert"), None),
        P(("dp", "expert")),
        P(("dp", "expert"), None),
        P(("dp", "expert"), None),
        P(("dp", "expert")),
        P(("dp", "expert"), None),
        P(("dp", "expert"), None),
        P(("dp", "expert"), None),
        P("expert", "dp", None),
        P("expert", "dp", None),
        P(("dp", "expert"), None),
        P("dp", None),
        P(("dp", "expert"), None),
    )
    return jax.shard_map(
        shards,
        mesh=mesh,
        in_specs=placed,
        out_specs=(
            P(("dp", "expert"), None),
            P(("dp", "expert"), None),
            P(("dp", "expert")),
            P(("dp", "expert"), None),
            P(("dp", "expert"), None),
            P(("dp", "expert")),
            P(("dp", "expert"), None),
            P(("dp", "expert"), None),
            P(("dp", "expert"), None),
            P("expert", "dp", None),
            P("expert", "dp", None),
        ),
        check_vma=False,
    )
```

profile of v0, /device:TPU:0, one launch (start us, length us, event | category | flops | bytes accessed | tf_op | source)
XLA Modules:
  0.0 1897.2 jit_solution(8463698940268162099)
XLA Ops:
  9.7 43.0 %all-reduce.5 = (bf16[1024]{0:T(1024)(128)(2,1)S(1)}, bf16[1024]{0:T(1024)(128)(2,1)S(1)}) all-reduce(bf16[1024]{0:T(1024)(128)(2,1)S(1)} %dynamic-update-slice, bf16[1024]{0:T(1024)(128)(2,1)S(1)} %dynamic-update-slice.1), channel_id=1, replica_groups=mesh['dp'=8,'expert'=4] {'dp','expert'}, use_global_device_ids=true, to_apply=%add | all-reduce | flops 2048 | bytes 8192
  55.0 28.4 %all-gather.11.cloned.1.call-done = bf16[1024,3072]{1,0:T(8,128)(2,1)} async-done(((bf16[32,3072]{1,0:T(8,128)(2,1)}), bf16[1024,3072]{1,0:T(8,128)(2,1)}) %all-gather.11.cloned.1.call-update) | async-done | bytes 6291472 | tf_op jit(solution)/shard_map/all_gather | solution.py:212
  91.5 65.9 %all-gather = bf16[32,32,2]{1,2,0:T(2,128)(2,1)S(1)} all-gather(bf16[1,32,2]{1,2,0:T(2,128)(2,1)S(1)} %bitcast.175), channel_id=1, replica_groups=mesh['dp'=8,'expert'=4] {'dp','expert'}, dimensions={0}, use_global_device_ids=true | all-gather | bytes 4224 | tf_op jit(solution)/shard_map/all_gather | solution.py:217
  168.2 23.2 %all-gather.15.cloned.1.call-done = bf16[1024,1024]{1,0:T(8,128)(2,1)} async-done(((bf16[32,1024]{1,0:T(8,128)(2,1)}), bf16[1024,1024]{1,0:T(8,128)(2,1)}) %all-gather.15.cloned.1.call-update) | async-done | bytes 2097168 | tf_op jit(solution)/shard_map/all_gather | solution.py:213
  200.8 45.6 %all-gather.21.cloned.1.call-done = bf16[1,1024,4096]{2,1,0:T(8,128)(2,1)} async-done(((bf16[1,128,4096]{2,1,0:T(8,128)(2,1)}), bf16[1,1024,4096]{2,1,0:T(8,128)(2,1)}) %all-gather.21.cloned.1.call-update) | async-done | bytes 8388624 | tf_op jit(solution)/shard_map/all_gather | solution.py:222
  255.0 47.6 %all-gather.23.cloned.1.call-done = bf16[1,4096,1024]{2,1,0:T(8,128)(2,1)} async-done(((bf16[1,512,1024]{2,1,0:T(8,128)(2,1)}), bf16[1,4096,1024]{2,1,0:T(8,128)(2,1)}) %all-gather.23.cloned.1.call-update) | async-done | bytes 8388624 | tf_op jit(solution)/shard_map/all_gather | solution.py:223
  302.6 6.9 fusion.56
  314.1 71.9 %all-gather.17.cloned.1.call-done = bf16[1024,4096]{1,0:T(8,128)(2,1)} async-done(((bf16[32,4096]{1,0:T(8,128)(2,1)}), bf16[1024,4096]{1,0:T(8,128)(2,1)}) %all-gather.17.cloned.1.call-update) | async-done | bytes 8388624 | tf_op jit(solution)/shard_map/all_gather | solution.py:218
  392.3 72.6 %all-gather.19.cloned.1.call-done = bf16[4096,1024]{1,0:T(8,128)(2,1)} async-done(((bf16[128,1024]{1,0:T(8,128)(2,1)}), bf16[4096,1024]{1,0:T(8,128)(2,1)}) %all-gather.19.cloned.1.call-update) | async-done | bytes 8388624 | tf_op jit(solution)/shard_map/all_gather | solution.py:219
  464.9 5.8 fusion.82
  477.7 8.0 fusion.38
  485.7 12.0 all-to-all-done.2
  497.7 8.7 fusion.16
  506.5 7.5 fusion.53
  517.5 7.4 fusion.136
  539.6 7.0 convert_bitcast_fusion
  546.7 7.4 fusion.8
  567.4 13.8 all_gather.60
  585.7 14.1 all_gather.62
  608.1 6.7 fusion.62
  614.8 7.4 fusion.86
  622.2 9.4 fusion.139
  632.3 8.2 fusion.96
  640.5 59.6 %reduce-scatter.22.cloned.1.call-done = f32[32,2]{1,0:T(8,128)} async-done(((f32[1024,2]{1,0:T(8,128)}), f32[32,2]{1,0:T(8,128)}) %reduce-scatter.22.cloned.1.call-update) | async-done | bytes 272
  701.5 5.1 fusion.80
  707.0 37.3 %all-reduce.4 = (f32[1024]{0:T(1024)S(1)}, f32[1024]{0:T(1024)S(1)}) all-reduce(f32[1024]{0:T(1024)S(1)} %get-tuple-element.108, f32[1024]{0:T(1024)S(1)} %copy-done.43), channel_id=2, replica_groups=mesh['dp'=8,'expert'=4] {'dp','expert'}, use_global_device_ids=true, to_apply=%region_21.22.clone | all-reduce | flops 2048 | bytes 16384
  746.4 25.9 %reduce-scatter.18.cloned.1.call-done = bf16[1,128,4096]{2,1,0:T(8,128)(2,1)} async-done(((bf16[1,1024,4096]{2,1,0:T(8,128)(2,1)}), bf16[1,128,4096]{2,1,0:T(8,128)(2,1)}) %reduce-scatter.18.cloned.1.call-update) | async-done | bytes 1048592 | tf_op jit(solution)/shard_map/reduce_scatter | solution.py:331
  775.0 71.9 %reduce-scatter.20.cloned.1.call-done = bf16[1,512,1024]{2,1,0:T(8,128)(2,1)} async-done(((bf16[1,4096,1024]{2,1,0:T(8,128)(2,1)}), bf16[1,512,1024]{2,1,0:T(8,128)(2,1)}) %reduce-scatter.20.cloned.1.call-update) | async-done | bytes 1048592 | tf_op jit(solution)/shard_map/reduce_scatter | solution.py:334
  849.7 147.6 %reduce-scatter.12.cloned.1.call-done = f32[32,1024]{1,0:T(8,128)} async-done(((f32[1024,1024]{1,0:T(8,128)}), f32[32,1024]{1,0:T(8,128)}) %reduce-scatter.12.cloned.1.call-update) | async-done | bytes 131088 | tf_op jit(solution)/shard_map/reduce_scatter | solution.py:400
  997.3 161.9 %reduce-scatter.10.cloned.1.call-done = f32[32,3072]{1,0:T(8,128)} async-done(((f32[1024,3072]{1,0:T(8,128)}), f32[32,3072]{1,0:T(8,128)}) %reduce-scatter.10.cloned.1.call-update) | async-done | bytes 393232 | tf_op jit(solution)/shard_map/reduce_scatter | solution.py:399
  1159.2 366.0 %reduce-scatter.14.cloned.1.call-done = f32[32,4096]{1,0:T(8,128)} async-done(((f32[1024,4096]{1,0:T(8,128)}), f32[32,4096]{1,0:T(8,128)}) %reduce-scatter.14.cloned.1.call-update) | async-done | bytes 524304 | tf_op jit(solution)/shard_map/reduce_scatter | solution.py:354
  1525.3 364.9 %reduce-scatter.16.cloned.1.call-done = f32[128,1024]{1,0:T(8,128)} async-done(((f32[4096,1024]{1,0:T(8,128)}), f32[128,1024]{1,0:T(8,128)}) %reduce-scatter.16.cloned.1.call-update) | async-done | bytes 524304 | tf_op jit(solution)/shard_map/reduce_scatter | solution.py:355
  (263 shorter events, 112.9 us)
Async XLA Ops:
  7.2 76.2 %all-gather.11.cloned.1.call-start = ((), (), s32[]{:S(2)}) async-start(), calls=%async_computation.11 | async-start | bytes 6488064 | tf_op jit(solution)/shard_map/all_gather | solution.py:212
  7.9 153.2 %all-gather.13.cloned.1.call-start = ((), (), s32[]{:S(2)}) async-start(), calls=%async_computation.12 | async-start | bytes 2621440 | tf_op jit(solution)/shard_map/all_gather | solution.py:233
  87.4 70.8 %copy-start.58 = (s32[128,1]{0,1:T(1,128)S(1)}, s32[128,1]{0,1:T(1,128)}, u32[]{:S(2)}) copy-start(s32[128,1]{0,1:T(1,128)} %param.23) | copy-start | bytes 1540
  87.4 71.1 %copy-start.71 = (s32[1,2]{1,0:T(1,128)S(1)}, s32[1,2]{1,0:T(1,128)}, u32[]{:S(2)}) copy-start(s32[1,2]{1,0:T(1,128)} %param.24) | copy-start | bytes 28
  88.2 103.2 %all-gather.15.cloned.1.call-start = ((), (), s32[]{:S(2)}) async-start(), calls=%async_computation.13 | async-start | bytes 2162688 | tf_op jit(solution)/shard_map/all_gather | solution.py:213
  89.0 157.5 %all-gather.21.cloned.1.call-start = ((), (), s32[]{:S(2)}) async-start(), calls=%async_computation.16 | async-start | bytes 9437184 | tf_op jit(solution)/shard_map/all_gather | solution.py:222
  89.6 213.0 %all-gather.23.cloned.1.call-start = ((), (), s32[]{:S(2)}) async-start(), calls=%async_computation.17 | async-start | bytes 9437184 | tf_op jit(solution)/shard_map/all_gather | solution.py:223
  90.2 295.8 %all-gather.17.cloned.1.call-start = ((), (), s32[]{:S(2)}) async-start(), calls=%async_computation.14 | async-start | bytes 8650752 | tf_op jit(solution)/shard_map/all_gather | solution.py:218
  90.7 374.2 %all-gather.19.cloned.1.call-start = ((), (), s32[]{:S(2)}) async-start(), calls=%async_computation.15 | async-start | bytes 8650752 | tf_op jit(solution)/shard_map/all_gather | solution.py:219
  91.5 469.6 %all-gather.25.cloned.1.call-start = ((), (), s32[]{:S(2)}) async-start(), calls=%async_computation.18 | async-start | bytes 1310720 | tf_op jit(solution)/shard_map/all_gather | solution.py:370
  193.6 57.9 %copy-start.44 = (f32[128]{0:T(128)}, f32[128]{0:T(128)S(1)}, u32[]{:S(2)}) copy-start(f32[128]{0:T(128)S(1)} %broadcast_multiply_fusion) | copy-start | bytes 1540
  195.9 50.6 %all-to-all-start = ((bf16[4,40,1024]{2,1,0:T(8,128)(2,1)}), bf16[4,40,1024]{2,1,0:T(8,128)(2,1)S(1)}, u32[]{:S(2)}, u32[]{:S(2)}) async-start(bf16[4,40,1024]{2,1,0:T(8,128)(2,1)} %bitcast.12), calls=%async_computation | async-start | bytes 655360 | tf_op jit(solution)/shard_map/all_to_all | solution.py:258
  200.2 51.3 %copy-start.45 = (f32[128,2]{0,1:T(2,128)}, f32[128,2]{0,1:T(2,128)S(1)}, u32[]{:S(2)}) copy-start(f32[128,2]{0,1:T(2,128)S(1)} %get-tuple-element.154) | copy-start | bytes 3076
  200.2 51.3 %copy-start.50 = (f32[128]{0:T(128)}, f32[128]{0:T(128)S(1)}, u32[]{:S(2)}) copy-start(f32[128]{0:T(128)S(1)} %get-tuple-element.153) | copy-start | bytes 1540
  309.5 81.1 %all-to-all-start.1 = ((bf16[4,40,1024]{2,1,0:T(8,128)(2,1)}), bf16[4,40,1024]{2,1,0:T(8,128)(2,1)S(1)}, u32[]{:S(2)}, u32[]{:S(2)}) async-start(bf16[4,40,1024]{2,1,0:T(8,128)(2,1)} %fusion.56), calls=%async_computation.1 | async-start | bytes 655360 | tf_op jit(solution)/shard_map/all_to_all | solution.py:266
  392.3 78.4 %copy-start.46 = (f32[128,2]{0,1:T(2,128)S(1)}, f32[128,2]{0,1:T(2,128)}, u32[]{:S(2)}) copy-start(f32[128,2]{0,1:T(2,128)} %copy-done.45) | copy-start | bytes 3076
  392.3 78.4 %copy-start.51 = (f32[128]{0:T(128)S(1)}, f32[128]{0:T(128)}, u32[]{:S(2)}) copy-start(f32[128]{0:T(128)} %copy-done.50) | copy-start | bytes 1540
  392.3 78.5 %copy-start.65 = (f32[128]{0:T(128)S(1)}, f32[128]{0:T(128)}, u32[]{:S(2)}) copy-start(f32[128]{0:T(128)} %fusion.108) | copy-start | bytes 1540
  392.3 79.0 %copy-start.10 = (bf16[128,1024]{1,0:T(8,128)(2,1)S(1)}, bf16[128,1024]{1,0:T(8,128)(2,1)}, u32[]{:S(2)}) copy-start(bf16[128,1024]{1,0:T(8,128)(2,1)} %param.25) | copy-start | bytes 786436
  473.4 24.3 %all-to-all-start.2 = ((bf16[4,40,1024]{2,1,0:T(8,128)(2,1)}), bf16[4,40,1024]{2,1,0:T(8,128)(2,1)}, u32[]{:S(2)}, u32[]{:S(2)}) async-start(bf16[4,40,1024]{2,1,0:T(8,128)(2,1)} %bitcast.148), calls=%async_computation.2 | async-start | bytes 655360 | tf_op jit(solution)/shard_map/all_to_all | solution.py:296
  514.0 14.1 all-to-all-start.3
  517.4 84.2 %all-gather.27.cloned.1.call-start = ((), (), s32[]{:S(2)}) async-start(), calls=%async_computation.19 | async-start | bytes 1310720 | tf_op jit(solution)/shard_map/all_gather | solution.py:371
  538.2 161.9 %reduce-scatter.22.cloned.1.call-start = ((), (), s32[]{:S(2)}) async-start(), calls=%async_computation.26 | async-start | bytes 540672
  539.6 232.7 %reduce-scatter.18.cloned.1.call-start = ((), (), s32[]{:S(2)}) async-start(), calls=%async_computation.24 | async-start | bytes 9437184 | tf_op jit(solution)/shard_map/reduce_scatter | solution.py:331
  546.7 300.2 %reduce-scatter.20.cloned.1.call-start = ((), (), s32[]{:S(2)}) async-start(), calls=%async_computation.25 | async-start | bytes 9437184 | tf_op jit(solution)/shard_map/reduce_scatter | solution.py:334
  554.2 443.1 %reduce-scatter.12.cloned.1.call-start = ((), (), s32[]{:S(2)}) async-start(), calls=%async_computation.21 | async-start | bytes 4325376 | tf_op jit(solution)/shard_map/reduce_scatter | solution.py:400
  558.0 601.2 %reduce-scatter.10.cloned.1.call-start = ((), (), s32[]{:S(2)}) async-start(), calls=%async_computation.20 | async-start | bytes 12976128 | tf_op jit(solution)/shard_map/reduce_scatter | solution.py:399
  622.2 903.1 %reduce-scatter.14.cloned.1.call-start = ((), (), s32[]{:S(2)}) async-start(), calls=%async_computation.22 | async-start | bytes 17301504 | tf_op jit(solution)/shard_map/reduce_scatter | solution.py:354
  631.6 1258.5 %reduce-scatter.16.cloned.1.call-start = ((), (), s32[]{:S(2)}) async-start(), calls=%async_computation.23 | async-start | bytes 17301504 | tf_op jit(solution)/shard_map/reduce_scatter | solution.py:355
  640.4 61.0 %copy-start.20 = (bf16[16,64,128]{2,1,0:T(8,128)(2,1)S(1)}, bf16[16,64,128]{2,1,0:T(8,128)(2,1)}, u32[]{:S(2)}) copy-start(bf16[16,64,128]{2,1,0:T(8,128)(2,1)} %copy-done.19) | copy-start | bytes 786436
  640.4 61.0 %copy-start.27 = (bf16[16,64,128]{2,1,0:T(8,128)(2,1)S(1)}, bf16[16,64,128]{2,1,0:T(8,128)(2,1)}, u32[]{:S(2)}) copy-start(bf16[16,64,128]{2,1,0:T(8,128)(2,1)} %copy-done.26) | copy-start | bytes 786436
  640.4 61.0 %copy-start.28 = (bf16[16,64,128]{2,1,0:T(8,128)(2,1)S(1)}, bf16[16,64,128]{2,1,0:T(8,128)(2,1)}, u32[]{:S(2)}) copy-start(bf16[16,64,128]{2,1,0:T(8,128)(2,1)} %fusion.62) | copy-start | bytes 786436
  (60 other events, 492.0 us)
Sparse Core Ops, SparseCore 0:
  10.9 72.4 all-gather.10
  88.4 44.5 all-gather.12
  135.9 55.4 all-gather.14
  193.2 53.2 all-gather.20
  248.2 54.3 all-gather.22
  305.4 80.5 all-gather.16
  388.9 75.9 all-gather.18
  466.5 34.0 all-gather.24
  538.3 25.9 all-gather.26
  566.4 133.6 reduce-scatter.21
  703.9 68.2 reduce-scatter.17
  775.6 71.2 reduce-scatter.19
  849.9 147.4 reduce-scatter.11
  1004.8 154.3 reduce-scatter.9
  1161.9 363.2 reduce-scatter.13
  1528.0 362.1 reduce-scatter.15
where the time goes:
time: 1900 us
  waiting for transfers between devices  1510 us (79%)
  blocking collectives  174 us (9%)
  matrix products  135 us (7%)
  local copies, waits for them, and re-layouts  25.8 us (1%)
  other arithmetic  23 us (1%)
    reduce_scatter x1, waiting for transfers between devices, shards(): lax.psum_scatter(grad_up, ('dp', 'expert'), scatter_dimension=0, tiled=True)  366 us
    reduce_scatter x1, waiting for transfers between devices, shards(): lax.psum_scatter(grad_down, ('dp', 'expert'), scatter_dimension=0, tiled=...  365 us
    reduce_scatter x1, waiting for transfers between devices, shards(): lax.psum_scatter(grad_qkv, ('dp', 'expert'), scatter_dimension=0, tiled=T...  162 us
    reduce_scatter x1, waiting for transfers between devices, shards(): lax.psum_scatter(grad_out_matrix, ('dp', 'expert'), scatter_dimension=0,...  148 us
    unnamed x2, blocking collectives  80.3 us
    all_gather x1, waiting for transfers between devices, shards(): lax.all_gather(w_down, ('dp', 'expert'), axis=0, tiled=True)  72.6 us
    reduce_scatter x1, waiting for transfers between devices, shards(): lax.psum_scatter(grad_expert_down[None].astype(jnp.bfloat16), 'dp', scatt...  71.9 us
    all_gather x1, waiting for transfers between devices, shards(): lax.all_gather(w_up, ('dp', 'expert'), axis=0, tiled=True)  71.9 us
  transfers between devices with their start and end apart: 20, of which 15 were waited for; matrix products, arithmetic and copies ran while one was open for 9% of the time, Pallas kernels for 0%

commit v1 on v0

v1 whole, which is shorter than its diff:
```python
import jax
import jax.numpy as jnp
from jax import lax
from jax.sharding import Mesh
from jax.sharding import PartitionSpec as P

HEAD_DIM = 64
EPSILON = 1e-05
SCORE_SCALE = 0.125
MASK_VALUE = -1e30
F32 = jnp.float32
BF16 = jnp.bfloat16
DP = ("chip", "core")
LANES = 128


def norm_parts(values):
    row_mean = jnp.mean(values, axis=-1, keepdims=True)
    centred = values - row_mean
    spread = jnp.mean(centred * centred, axis=-1, keepdims=True)
    inverse = lax.rsqrt(spread + EPSILON)
    return (centred * inverse, inverse)


def norm_back(grad, normed, inverse, gain):
    scaled = grad * gain
    return inverse * (
        scaled
        - jnp.mean(scaled, axis=-1, keepdims=True)
        - normed * jnp.mean(scaled * normed, axis=-1, keepdims=True)
    )


def smooth(values):
    return jax.nn.gelu(values, approximate=True)


def smooth_back(values, grad):
    return jax.vjp(smooth, values)[1](grad)[0]


def dot(left, right):
    return jnp.dot(left, right, preferred_element_type=F32)


def dot_rt(left, right):
    return lax.dot_general(left, right, (((1,), (1,)), ((), ())), preferred_element_type=F32)


def dot_lt(left, right):
    return lax.dot_general(left, right, (((0,), (0,)), ((), ())), preferred_element_type=F32)


def gather(values, axes):
    return lax.all_gather(values, axes, axis=0, tiled=True)


def scatter_sum(values, axes):
    return lax.psum_scatter(values, axes, scatter_dimension=0, tiled=True)


def swap(values, axis):
    return lax.all_to_all(values, axis, split_axis=0, concat_axis=0, tiled=True)


def other_core(values):
    return lax.ppermute(values, "core", [(0, 1), (1, 0)])


def high_low(values):
    high = values.astype(BF16)
    return (high, (values - high.astype(F32)).astype(BF16))


def shards(
    tokens,
    first_gain,
    w_qkv,
    w_out,
    second_gain,
    w_mix,
    w_up,
    w_down,
    expert_up,
    expert_down,
    expert_ids,
    doc_lengths,
    out_grad,
):
    rows, width = tokens.shape
    n_chip, n_core, n_exp = (lax.axis_size(a) for a in ("chip", "core", "expert"))
    n_dp = n_chip * n_core
    group = rows * n_exp
    heads = width // HEAD_DIM // n_exp
    head_cols = heads * HEAD_DIM
    w_rows = w_qkv.shape[0]
    dense_rows = w_down.shape[0]
    dense_cols = n_dp * dense_rows
    exp_rows = expert_up.shape[1]
    exp_cols = expert_down.shape[1]
    ex = lax.axis_index("expert")
    core = lax.axis_index("core")
    start = ex * rows
    capacity = n_exp * max(2, 5 * rows // (4 * n_exp))

    exp_split = (
        expert_up[0]
        .reshape(exp_rows, n_chip, n_core, exp_cols)
        .transpose(2, 0, 1, 3)
        .reshape(n_core, exp_rows, n_chip * exp_cols)
    )
    own_half = jnp.where(core == 0, exp_split[0], exp_split[1])
    sent_half = jnp.where(core == 0, exp_split[1], exp_split[0])
    got_half = other_core(sent_half)
    chip_up = jnp.concatenate(
        [jnp.where(core == 0, own_half, got_half), jnp.where(core == 0, got_half, own_half)], axis=0
    )
    up_expert = gather(chip_up, "chip")
    down_expert = gather(expert_down[0], "chip")

    qkv_blocks = (
        w_qkv.reshape(w_rows, 3, n_exp, head_cols)
        .transpose(2, 0, 1, 3)
        .reshape(n_exp, w_rows, 3 * head_cols)
    )
    small = jnp.concatenate([first_gain[:, None], second_gain[:, None], w_mix], axis=1)
    small = jnp.pad(small, ((0, 0), (0, LANES - 4)))
    small = jnp.broadcast_to(small[None], (n_exp, w_rows, LANES))
    up_blocks = (
        w_up.reshape(w_rows, n_dp, n_exp, dense_rows)
        .transpose(2, 0, 1, 3)
        .reshape(n_exp, w_rows, dense_cols)
    )
    dealt = swap(jnp.concatenate([qkv_blocks, small, up_blocks], axis=2), "expert")
    dealt = dealt.reshape(n_exp * w_rows, 3 * head_cols + LANES + dense_cols)
    first_all = gather(dealt[:, : 3 * head_cols + LANES], DP)
    qkv_matrix = first_all[:, : 3 * head_cols]
    small_all = first_all[:, 3 * head_cols : 3 * head_cols + 4].astype(F32)
    gain_one = small_all[:, 0][None, :]
    gain_two = small_all[:, 1][None, :]
    mix_matrix = first_all[:, 3 * head_cols + 2 : 3 * head_cols + 4]
    mix_rows = small_all[:, 2:4].T
    up_matrix = gather(dealt[:, 3 * head_cols + LANES :], DP)
    down_matrix = gather(w_down, DP)
    out_matrix = gather(w_out, ("chip", "core", "expert"))

    inputs = gather(tokens, "expert").astype(F32)
    id_row = jnp.pad(expert_ids[:, 0].astype(BF16)[None], ((0, 7), (0, width - rows)))
    grad_pack = gather(jnp.concatenate([out_grad, id_row], axis=0), "expert")
    grad_pack = grad_pack.reshape(n_exp, rows + 8, width)
    grad_low = grad_pack[:, :rows].reshape(group, width)
    choice = grad_pack[:, rows, :rows].reshape(group)
    grad_output = grad_low.astype(F32)

    normed_one, inverse_one = norm_parts(inputs)
    attn_input = (normed_one * gain_one).astype(BF16)
    qkv = dot(attn_input, qkv_matrix).astype(BF16)
    query = qkv[:, :head_cols].reshape(group, heads, HEAD_DIM)
    keys = qkv[:, head_cols : 2 * head_cols].reshape(group, heads, HEAD_DIM)
    vals = qkv[:, 2 * head_cols :].reshape(group, heads, HEAD_DIM)
    doc_split = doc_lengths[0, 0]
    place = jnp.arange(group, dtype=jnp.int32)
    allowed = (place[:, None] >= place[None, :]) & (
        (place[:, None] >= doc_split) == (place[None, :] >= doc_split)
    )
    scores = jnp.einsum("qhd,khd->hqk", query, keys, preferred_element_type=F32) * SCORE_SCALE
    probs = jax.nn.softmax(jnp.where(allowed[None], scores, MASK_VALUE), axis=-1)
    probs_low = probs.astype(BF16)
    attended_own = jnp.einsum("hqk,khd->qhd", probs_low, vals, preferred_element_type=F32)
    attended_own = attended_own.reshape(group, head_cols).astype(BF16)
    attended = lax.all_gather(attended_own, "expert", axis=1, tiled=True)

    middle = inputs + dot(attended, out_matrix)
    normed_two, inverse_two = norm_parts(middle)
    ffn_input = (normed_two * gain_two).astype(BF16)
    coeffs = jax.nn.softmax(dot(ffn_input, mix_matrix), axis=-1)

    ddense = (coeffs[:, 0:1] * grad_output).astype(BF16)
    dexpert = (coeffs[:, 1:2] * grad_output).astype(BF16)
    dense_pre = dot(ffn_input, up_matrix)
    dense_act = smooth(dense_pre).astype(BF16)
    dense_part = dot(dense_act, down_matrix)
    dense_dpre = smooth_back(dense_pre, dot_rt(ddense, down_matrix)).astype(BF16)
    dffn_part = dot_rt(dense_dpre, up_matrix)
    down_part = dot_lt(dense_act, ddense).astype(BF16)
    up_part = dot_lt(ffn_input, dense_dpre).astype(BF16)

    chosen = choice == ex.astype(BF16)
    slot = jnp.where(chosen, jnp.cumsum(chosen.astype(jnp.int32)) - 1, -1)
    pick = (jnp.arange(capacity, dtype=jnp.int32)[:, None] == slot[None, :]).astype(BF16)
    rows_in = dot(pick, ffn_input).astype(BF16)
    rows_grad = dot(pick, dexpert).astype(BF16)
    pair = other_core(jnp.concatenate([rows_in, rows_grad], axis=1))
    rows_in = jnp.concatenate([rows_in, pair[:, :width]], axis=0)
    rows_grad = jnp.concatenate([rows_grad, pair[:, width:]], axis=0)
    exp_pre = dot(rows_in, up_expert)
    exp_act = smooth(exp_pre).astype(BF16)
    exp_part = dot(exp_act, down_expert)
    exp_dpre = smooth_back(exp_pre, dot_rt(rows_grad, down_expert)).astype(BF16)
    din_part = dot_rt(exp_dpre, up_expert)
    back = jnp.concatenate([exp_part[capacity:], din_part[capacity:]], axis=1).astype(BF16)
    back = other_core(back).astype(F32)
    exp_out = (exp_part[:capacity] + back[:, :width]).astype(BF16)
    exp_din = (din_part[:capacity] + back[:, width:]).astype(BF16)
    exp_rows_all = dot_lt(pick, exp_out)
    din_all = dot_lt(pick, exp_din)
    down_exp_part = dot_lt(exp_act, rows_grad).astype(BF16)
    up_exp_part = dot_lt(rows_in, exp_dpre).astype(BF16)

    dffn_part = dffn_part + din_all
    dcoeff = [
        jnp.sum(grad_output * dense_part, axis=1).reshape(n_exp, rows),
        jnp.sum(grad_output * exp_rows_all, axis=1).reshape(n_exp, rows),
    ]
    extra = jnp.concatenate([p for d in dcoeff for p in high_low(d)], axis=1)
    extra = jnp.pad(extra[:, None, :], ((0, 0), (0, 7), (0, width - 4 * rows)))
    payload = jnp.concatenate([dffn_part.astype(BF16).reshape(n_exp, rows, width), extra], axis=1)
    arrived = jnp.sum(swap(payload, "expert").astype(F32), axis=0)
    dffn = arrived[:rows]
    tail = arrived[rows]
    dcoeffs = jnp.stack(
        [tail[:rows] + tail[rows : 2 * rows], tail[2 * rows : 3 * rows] + tail[3 * rows : 4 * rows]],
        axis=1,
    )
    out_part = (coeffs[:, 0:1] * dense_part + coeffs[:, 1:2] * exp_rows_all).astype(BF16)
    out_sum = jnp.sum(swap(out_part.reshape(n_exp, rows, width), "expert").astype(F32), axis=0)

    def mine(values):
        return lax.dynamic_slice_in_dim(values, start, rows, 0)

    output = (mine(middle) + out_sum).astype(BF16)
    coeffs_own = mine(coeffs)
    dlogits = (
        coeffs_own * (dcoeffs - jnp.sum(coeffs_own * dcoeffs, axis=1, keepdims=True))
    ).astype(BF16)
    dlog = dlogits.astype(F32)
    dffn = dffn + dlog[:, 0:1] * mix_rows[0:1] + dlog[:, 1:2] * mix_rows[1:2]
    normed_own = mine(normed_two)
    dmiddle = out_grad.astype(F32) + norm_back(dffn, normed_own, mine(inverse_two), gain_two)
    gain_two_part = jnp.sum(dffn * normed_own, axis=0)
    mix_part = dot_lt(mine(ffn_input), dlogits)
    dmid_low = dmiddle.astype(BF16)
    out_weight_part = dot_lt(mine(attended), dmid_low).astype(BF16)
    dattended = dot_rt(dmid_low, out_matrix).astype(BF16)
    dattended = swap(
        dattended.reshape(rows, n_exp, head_cols).transpose(1, 0, 2), "expert"
    ).reshape(group, heads, HEAD_DIM)

    dprobs = jnp.einsum("qhd,khd->hqk", dattended, vals, preferred_element_type=F32)
    delta = jnp.sum(probs * dprobs, axis=-1, keepdims=True)
    dscores = (probs * (dprobs - delta)).astype(BF16)
    dquery = jnp.einsum("hqk,khd->qhd", dscores, keys, preferred_element_type=F32) * SCORE_SCALE
    dkeys = jnp.einsum("hqk,qhd->khd", dscores, query, preferred_element_type=F32) * SCORE_SCALE
    dvals = jnp.einsum("hqk,qhd->khd", probs_low, dattended, preferred_element_type=F32)
    dqkv = jnp.concatenate(
        [g.reshape(group, head_cols) for g in (dquery, dkeys, dvals)], axis=1
    ).astype(BF16)
    dattn_part = dot_rt(dqkv, qkv_matrix)
    gain_one_part = jnp.sum(dattn_part * normed_one, axis=0)
    qkv_part = dot_lt(attn_input, dqkv).astype(BF16)
    dattn = jnp.sum(
        swap(dattn_part.astype(BF16).reshape(n_exp, rows, width), "expert").astype(F32), axis=0
    )
    tokens_grad = (
        dmiddle + norm_back(dattn, mine(normed_one), mine(inverse_one), gain_one)
    ).astype(BF16)

    up_exp_sum = scatter_sum(up_exp_part, "chip")
    down_exp_sum = scatter_sum(down_exp_part, "chip")
    own_rows = jnp.where(core == 0, up_exp_sum[:exp_rows], up_exp_sum[exp_rows:])
    sent_rows = jnp.where(core == 0, up_exp_sum[exp_rows:], up_exp_sum[:exp_rows])
    got_rows = other_core(sent_rows)
    exp_up_grad = jnp.stack(
        [jnp.where(core == 0, own_rows, got_rows), jnp.where(core == 0, got_rows, own_rows)], axis=0
    ).reshape(n_core, exp_rows, n_chip, exp_cols)
    exp_up_grad = exp_up_grad.transpose(1, 2, 0, 3).reshape(1, exp_rows, n_dp * exp_cols)
    down_sum = scatter_sum(down_part, DP)
    up_sum = scatter_sum(up_part, DP)
    up_sum = swap(up_sum.reshape(n_exp, w_rows, dense_cols), "expert")
    up_sum = (
        up_sum.reshape(n_exp, w_rows, n_dp, dense_rows)
        .transpose(1, 2, 0, 3)
        .reshape(w_rows, n_exp * dense_cols)
    )
    out_weight_sum = scatter_sum(scatter_sum(out_weight_part, DP), "expert")
    small_part = jnp.concatenate([gain_one_part[:, None], gain_two_part[:, None], mix_part], axis=1)
    small_part = jnp.pad(small_part.astype(BF16), ((0, 0), (0, LANES - 4)))
    qkv_sum = scatter_sum(jnp.concatenate([qkv_part, small_part], axis=1), DP)
    qkv_sum = swap(qkv_sum.reshape(n_exp, w_rows, 3 * head_cols + LANES), "expert").astype(F32)
    small_sum = jnp.sum(qkv_sum[:, :, 3 * head_cols : 3 * head_cols + 4], axis=0)
    qkv_sum = (
        qkv_sum[:, :, : 3 * head_cols]
        .reshape(n_exp, w_rows, 3, head_cols)
        .transpose(1, 2, 0, 3)
        .reshape(w_rows, 3 * width)
    )
    return (
        output,
        tokens_grad,
        small_sum[:, 0],
        qkv_sum,
        out_weight_sum.astype(F32),
        small_sum[:, 1],
        small_sum[:, 2:4],
        up_sum.astype(F32),
        down_sum.astype(F32),
        exp_up_grad.astype(F32),
        down_exp_sum.astype(F32)[None],
    )


def solution(mesh):
    n_dp, n_exp = (mesh.shape["dp"], mesh.shape["expert"])
    fine = Mesh(mesh.devices.reshape(n_dp // 2, 2, n_exp), ("chip", "core", "expert"))
    every = ("chip", "core", "expert")
    by_rows = P(every, None)
    by_expert = P("expert", DP, None)
    return jax.shard_map(
        shards,
        mesh=fine,
        in_specs=(
            by_rows,
            P(every),
            by_rows,
            by_rows,
            P(every),
            by_rows,
            by_rows,
            by_rows,
            by_expert,
            by_expert,
            by_rows,
            P(DP, None),
            by_rows,
        ),
        out_specs=(
            by_rows,
            by_rows,
            P(every),
            by_rows,
            by_rows,
            P(every),
            by_rows,
            by_rows,
            by_rows,
            by_expert,
            by_expert,
        ),
        check_vma=False,
    )
```

time: 1900 us -> 746 us (0.39)
  waiting for transfers between devices: 1510 us -> 482 us
  blocking collectives: 174 us -> 72.2 us
  matrix products: 135 us -> 79.8 us
    reduce_scatter x6 -> x7, waiting for transfers between devices: 1140 us -> 180 us  [scatter_sum(): return lax.psum_scatter(values, axes, scatter_dimension=0, tiled=True)]
    all_gather x3 -> x0, blocking collectives: 93.9 us -> none  [the longest x1 65.9 us: shards(): lax.all_gather(w_mix, ('dp', 'expert'), axis=0, tiled=True)]
    unnamed x2 -> x0, blocking collectives: 80.3 us -> none
    all_to_all x0 -> x3, blocking collectives: none -> 72.2 us  [swap(): return lax.all_to_all(values, axis, split_axis=0, concat_axis=0, tiled=True)]
    unnamed x17 -> x16, waiting for transfers between devices: 63.4 us -> 2.6 us
    dot_general x27 -> x29, matrix products: 134 us -> 76.1 us  [the longest x9 27.5 us: dot_lt(): lax.dot_general(left, right, (((0,), (0,)), ((), ())), preferred_element_...]
    all_gather x9, waiting for transfers between devices: 289 us -> 258 us  [the longest x8 230 us: gather(): return lax.all_gather(values, axes, axis=0, tiled=True)]
    all_to_all x4, waiting for transfers between devices: 15.2 us -> 37.2 us  [swap(): return lax.all_to_all(values, axis, split_axis=0, concat_axis=0, tiled=True)]
  transfers between devices with their start and end apart: 20 -> 24, of which waited for: 15 -> 20; matrix products, arithmetic and copies ran while one was open for 9% -> 16% of each run, Pallas kernels for 0% -> 0%
where the time goes in v1:
time: 746 us; the launch traced here: 738 us
  waiting for transfers between devices  482 us (65%)
  matrix products  79.8 us (11%)
  blocking collectives  72.2 us (10%)
  local copies, waits for them, and re-layouts  36.3 us (5%)
  other arithmetic  33.9 us (5%)
  starting transfers between devices  18.7 us (3%)
  between operations  15.4 us (2%)
    all_gather x8, waiting for transfers between devices, gather(): return lax.all_gather(values, axes, axis=0, tiled=True)  230 us
    reduce_scatter x7, waiting for transfers between devices, scatter_sum(): return lax.psum_scatter(values, axes, scatter_dimension=0, tiled=True)  180 us
    all_to_all x3, blocking collectives, swap(): return lax.all_to_all(values, axis, split_axis=0, concat_axis=0, tiled=True)  72.2 us
    all_to_all x4, waiting for transfers between devices, swap(): return lax.all_to_all(values, axis, split_axis=0, concat_axis=0, tiled=True)  37.2 us
    all_gather x1, waiting for transfers between devices, shards(): attended = lax.all_gather(attended_own, 'expert', axis=1, tiled=True)  28.8 us
    dot_general x9, matrix products, dot_lt(): lax.dot_general(left, right, (((0,), (0,)), ((), ())), preferred_element_...  27.5 us
    dot_general x9, matrix products, dot(): return jnp.dot(left, right, preferred_element_type=F32)  22.9 us
    all_to_all x4, starting transfers between devices, swap(): return lax.all_to_all(values, axis, split_axis=0, concat_axis=0, tiled=True)  17 us
  transfers between devices with their start and end apart: 24, of which 20 were waited for; matrix products, arithmetic and copies ran while one was open for 16% of the time, Pallas kernels for 0%

profile of v1, /device:TPU:0, one launch (start us, length us, event | category | flops | bytes accessed | tf_op | source)
XLA Modules:
  0.0 738.5 jit_solution(12629946359078659122)
XLA Ops:
  10.9 30.9 %all_to_all.35 = bf16[4,32,1920]{2,1,0:T(8,128)(2,1)S(1)} all-to-all(bf16[4,32,1920]{2,1,0:T(8,128)(2,1)S(1)} %pad_maximum_fusion.7), channel_id=1, replica_groups=mesh['chip'=4,'core'=2,'expert'=4] {'expert'}, dimensions={0} | all-to-all | bytes 983040 | tf_op jit(solution)/shard_map/all_to_all | solution.py:63
  51.3 25.4 %all-gather.13.cloned.1.call-done = bf16[1024,896]{0,1:T(8,128)(2,1)} async-done(((bf16[128,896]{0,1:T(8,128)(2,1)}), bf16[1024,896]{0,1:T(8,128)(2,1)}) %all-gather.13.cloned.1.call-update) | async-done | bytes 1835024 | tf_op jit(solution)/shard_map/all_gather | solution.py:55
  84.1 3.6 convolution_convert_fusion.11
  94.8 13.1 %all-gather.23.cloned.1.call-done = bf16[544,1024]{1,0:T(8,128)(2,1)} async-done(((bf16[136,1024]{1,0:T(8,128)(2,1)}), bf16[544,1024]{1,0:T(8,128)(2,1)}) %all-gather.23.cloned.1.call-update) | async-done | bytes 1114128 | tf_op jit(solution)/shard_map/all_gather | solution.py:55
  111.5 55.2 %all-gather.17.cloned.1.call-done = bf16[1024,1024]{1,0:T(8,128)(2,1)} async-done(((bf16[32,1024]{1,0:T(8,128)(2,1)}), bf16[1024,1024]{1,0:T(8,128)(2,1)}) %all-gather.17.cloned.1.call-update) | async-done | bytes 2097168 | tf_op jit(solution)/shard_map/all_gather | solution.py:55
  166.7 28.8 %all-gather.15.cloned.1.call-done = bf16[512,1024]{0,1:T(8,128)(2,1)} async-done(((bf16[512,256]{0,1:T(8,128)(2,1)}), bf16[512,1024]{0,1:T(8,128)(2,1)}) %all-gather.15.cloned.1.call-update) | async-done | bytes 1048592 | tf_op jit(solution)/shard_map/all_gather | solution.py:171
  208.9 41.1 %all-gather.25.cloned.1.call-done = bf16[1024,2048]{1,0:T(8,128)(2,1)} async-done(((bf16[256,2048]{1,0:T(8,128)(2,1)}), bf16[1024,2048]{1,0:T(8,128)(2,1)}) %all-gather.25.cloned.1.call-update) | async-done | bytes 4194320 | tf_op jit(solution)/shard_map/all_gather | solution.py:55
  250.0 5.3 fusion.53
  255.3 49.3 %all-gather.27.cloned.1.call-done = bf16[1,2048,1024]{2,1,0:T(8,128)(2,1)} async-done(((bf16[1,512,1024]{2,1,0:T(8,128)(2,1)}), bf16[1,2048,1024]{2,1,0:T(8,128)(2,1)}) %all-gather.27.cloned.1.call-update) | async-done | bytes 4194320 | tf_op jit(solution)/shard_map/all_gather | solution.py:55
  304.6 6.3 fusion.12
  318.0 16.9 %all-gather.19.cloned.1.call-done = bf16[1024,1024]{1,0:T(8,128)(2,1)} async-done(((bf16[128,1024]{1,0:T(8,128)(2,1)}), bf16[1024,1024]{1,0:T(8,128)(2,1)}) %all-gather.19.cloned.1.call-update) | async-done | bytes 2097168 | tf_op jit(solution)/shard_map/all_gather | solution.py:55
  335.0 4.2 fusion.98
  339.1 25.7 %all-gather.21.cloned.1.call-done = bf16[1024,1024]{1,0:T(8,128)(2,1)} async-done(((bf16[128,1024]{1,0:T(8,128)(2,1)}), bf16[1024,1024]{1,0:T(8,128)(2,1)}) %all-gather.21.cloned.1.call-update) | async-done | bytes 2097168 | tf_op jit(solution)/shard_map/all_gather | solution.py:55
  364.8 3.9 fusion.86
  378.4 4.6 all-to-all-start.2
  383.1 27.5 %all-to-all-done.2 = bf16[4,136,1024]{2,1,0:T(8,128)(2,1)} async-done(((bf16[4,136,1024]{2,1,0:T(8,128)(2,1)}), bf16[4,136,1024]{2,1,0:T(8,128)(2,1)}, u32[]{:S(2)}, u32[]{:S(2)}) %all-to-all-start.2) | async-done | bytes 1114144 | tf_op jit(solution)/shard_map/all_to_all | solution.py:63
  418.9 3.9 convolution_convert_fusion.3
  426.2 4.0 all-to-all-start.3
  430.3 4.7 convolution_convert_fusion.2
  453.7 3.9 copy.143
  457.7 5.7 convolution_convert_fusion.1
  464.4 6.4 convolution_convert_fusion
  472.0 27.9 %all_to_all.36 = bf16[4,128,1024]{2,1,0:T(8,128)(2,1)} all-to-all(bf16[4,128,1024]{2,1,0:T(8,128)(2,1)S(1)} %bitcast.150), channel_id=1, replica_groups=mesh['chip'=4,'core'=2,'expert'=4] {'expert'}, dimensions={0} | all-to-all | bytes 2097152 | tf_op jit(solution)/shard_map/all_to_all | solution.py:63
  503.2 13.5 %all_to_all.37 = bf16[4,32,1024]{2,1,0:T(8,128)(2,1)S(1)} all-to-all(bf16[4,32,1024]{2,1,0:T(8,128)(2,1)} %bitcast.180), channel_id=1, replica_groups=mesh['chip'=4,'core'=2,'expert'=4] {'expert'}, dimensions={0} | all-to-all | bytes 524288 | tf_op jit(solution)/shard_map/all_to_all | solution.py:63
  516.7 3.8 all-to-all-start.4
  522.8 24.8 %reduce-scatter.16.cloned.1.call-done = bf16[128,1024]{1,0:T(8,128)(2,1)} async-done(((bf16[1024,1024]{1,0:T(8,128)(2,1)}), bf16[128,1024]{1,0:T(8,128)(2,1)}) %reduce-scatter.16.cloned.1.call-update) | async-done | bytes 262160 | tf_op jit(solution)/shard_map/reduce_scatter | solution.py:59
  552.2 38.8 %reduce-scatter.22.cloned.1.call-done = bf16[128,896]{1,0:T(8,128)(2,1)} async-done(((bf16[1024,896]{1,0:T(8,128)(2,1)}), bf16[128,896]{1,0:T(8,128)(2,1)}) %reduce-scatter.22.cloned.1.call-update) | async-done | bytes 229392 | tf_op jit(solution)/shard_map/reduce_scatter | solution.py:59
  591.1 4.6 all-to-all-start.5
  597.6 6.3 all-to-all-done.5
  605.4 41.5 %reduce-scatter.18.cloned.1.call-done = bf16[256,2048]{1,0:T(8,128)(2,1)} async-done(((bf16[1024,2048]{1,0:T(8,128)(2,1)}), bf16[256,2048]{1,0:T(8,128)(2,1)}) %reduce-scatter.18.cloned.1.call-update) | async-done | bytes 1048592 | tf_op jit(solution)/shard_map/reduce_scatter | solution.py:59
  649.7 19.0 %reduce-scatter.12.cloned.1.call-done = bf16[32,1024]{1,0:T(8,128)(2,1)} async-done(((bf16[128,1024]{1,0:T(8,128)(2,1)}), bf16[32,1024]{1,0:T(8,128)(2,1)}) %reduce-scatter.12.cloned.1.call-update) | async-done | bytes 65552 | tf_op jit(solution)/shard_map/reduce_scatter | solution.py:59
  670.2 52.6 %reduce-scatter.20.cloned.1.call-done = bf16[512,1024]{1,0:T(8,128)(2,1)} async-done(((bf16[2048,1024]{1,0:T(8,128)(2,1)}), bf16[512,1024]{1,0:T(8,128)(2,1)}) %reduce-scatter.20.cloned.1.call-update) | async-done | bytes 1048592 | tf_op jit(solution)/shard_map/reduce_scatter | solution.py:59
  (260 shorter events, 120.1 us)
Async XLA Ops:
  7.2 40.9 %all-gather.11.cloned.1.call-start = ((), (), s32[]{:S(2)}) async-start(), calls=%async_computation.14 | async-start | bytes 1310720 | tf_op jit(solution)/shard_map/all_gather | solution.py:55
  7.9 68.8 %all-gather.13.cloned.1.call-start = ((), (), s32[]{:S(2)}) async-start(), calls=%async_computation.15 | async-start | bytes 2064384 | tf_op jit(solution)/shard_map/all_gather | solution.py:55
  10.3 33.2 %copy-start.36 = (s32[128,1]{0,1:T(1,128)S(1)}, s32[128,1]{0,1:T(1,128)}, u32[]{:S(2)}) copy-start(s32[128,1]{0,1:T(1,128)} %param.23) | copy-start | bytes 1540
  10.4 33.2 %copy-start.16 = (bf16[128,1024]{1,0:T(8,128)(2,1)S(1)}, bf16[128,1024]{1,0:T(8,128)(2,1)}, u32[]{:S(2)}) copy-start(bf16[128,1024]{1,0:T(8,128)(2,1)} %param.25) | copy-start | bytes 786436
  10.7 34.3 %copy-start.37 = (s32[1,2]{1,0:T(1,128)S(1)}, s32[1,2]{1,0:T(1,128)}, u32[]{:S(2)}) copy-start(s32[1,2]{1,0:T(1,128)} %param.24) | copy-start | bytes 28
  43.5 64.4 %all-gather.23.cloned.1.call-start = ((), (), s32[]{:S(2)}) async-start(), calls=%async_computation.20 | async-start | bytes 1392640 | tf_op jit(solution)/shard_map/all_gather | solution.py:55
  44.3 122.3 %all-gather.17.cloned.1.call-start = ((), (), s32[]{:S(2)}) async-start(), calls=%async_computation.17 | async-start | bytes 2162688 | tf_op jit(solution)/shard_map/all_gather | solution.py:55
  44.9 150.6 %all-gather.15.cloned.1.call-start = ((), (), s32[]{:S(2)}) async-start(), calls=%async_computation.16 | async-start | bytes 1310720 | tf_op jit(solution)/shard_map/all_gather | solution.py:171
  48.1 29.4 %copy-start = (bf16[512,1024]{1,0:T(8,128)(2,1)S(1)}, bf16[512,1024]{1,0:T(8,128)(2,1)}, u32[]{:S(2)}) copy-start(bf16[512,1024]{1,0:T(8,128)(2,1)} %all-gather.11.cloned.1.call-done) | copy-start | bytes 3145732
  87.8 162.2 %all-gather.25.cloned.1.call-start = ((), (), s32[]{:S(2)}) async-start(), calls=%async_computation.21 | async-start | bytes 5242880 | tf_op jit(solution)/shard_map/all_gather | solution.py:55
  89.6 2.0 collective-permute-start.1
  92.8 211.8 %all-gather.27.cloned.1.call-start = ((), (), s32[]{:S(2)}) async-start(), calls=%async_computation.28 | async-start | bytes 5242880 | tf_op jit(solution)/shard_map/all_gather | solution.py:55
  93.5 241.4 %all-gather.19.cloned.1.call-start = ((), (), s32[]{:S(2)}) async-start(), calls=%async_computation.18 | async-start | bytes 2359296 | tf_op jit(solution)/shard_map/all_gather | solution.py:55
  94.3 270.4 %all-gather.21.cloned.1.call-start = ((), (), s32[]{:S(2)}) async-start(), calls=%async_computation.19 | async-start | bytes 2359296 | tf_op jit(solution)/shard_map/all_gather | solution.py:55
  204.5 2.4 collective-permute-start
  304.6 6.3 copy-start.32
  318.0 50.7 %collective-permute-start.2 = (bf16[160,2048]{1,0:T(8,128)(2,1)}, bf16[160,2048]{1,0:T(8,128)(2,1)}, u32[]{:S(2)}, u32[]{:S(2)}) collective-permute-start(bf16[160,2048]{1,0:T(8,128)(2,1)} %pad_maximum_fusion.6), channel_id=1, source_target_pairs={{0,4},{4,0},{1,5},{5,1},{2,6},{6,2},{3,7},{7,3},{8,12},{12,8},{9,1... | collective-permute-start | bytes 1966088 | tf_op jit(solution)/shard_map/ppermute | solution.py:67
  364.8 5.3 copy-start.20
  378.4 32.3 %all-to-all-start.2 = ((bf16[4,136,1024]{2,1,0:T(8,128)(2,1)}), bf16[4,136,1024]{2,1,0:T(8,128)(2,1)}, u32[]{:S(2)}, u32[]{:S(2)}) async-start(bf16[4,136,1024]{2,1,0:T(8,128)(2,1)} %fusion.38), calls=%async_computation.2 | async-start | bytes 2228224 | tf_op jit(solution)/shard_map/all_to_all | solution.py:63
  383.0 80.4 %reduce-scatter.10.cloned.1.call-start = ((), (), s32[]{:S(2)}) async-start(), calls=%async_computation.22 | async-start | bytes 2359296 | tf_op jit(solution)/shard_map/reduce_scatter | solution.py:59
  418.8 84.4 %reduce-scatter.14.cloned.1.call-start = ((), (), s32[]{:S(2)}) async-start(), calls=%async_computation.24 | async-start | bytes 2359296 | tf_op jit(solution)/shard_map/reduce_scatter | solution.py:59
  426.2 12.6 %all-to-all-start.3 = ((bf16[4,128,256]{2,1,0:T(8,128)(2,1)}), bf16[4,128,256]{2,1,0:T(8,128)(2,1)}, u32[]{:S(2)}, u32[]{:S(2)}) async-start(bf16[4,128,256]{2,1,0:T(8,128)(2,1)} %bitcast.168), calls=%async_computation.3 | async-start | bytes 524288 | tf_op jit(solution)/shard_map/all_to_all | solution.py:63
  430.3 117.3 %reduce-scatter.16.cloned.1.call-start = ((), (), s32[]{:S(2)}) async-start(), calls=%async_computation.25 | async-start | bytes 2359296 | tf_op jit(solution)/shard_map/reduce_scatter | solution.py:59
  435.0 156.0 %reduce-scatter.22.cloned.1.call-start = ((), (), s32[]{:S(2)}) async-start(), calls=%async_computation.29 | async-start | bytes 2064384 | tf_op jit(solution)/shard_map/reduce_scatter | solution.py:59
  457.6 189.3 %reduce-scatter.18.cloned.1.call-start = ((), (), s32[]{:S(2)}) async-start(), calls=%async_computation.26 | async-start | bytes 5242880 | tf_op jit(solution)/shard_map/reduce_scatter | solution.py:59
  463.4 205.3 %reduce-scatter.12.cloned.1.call-start = ((), (), s32[]{:S(2)}) async-start(), calls=%async_computation.23 | async-start | bytes 327680 | tf_op jit(solution)/shard_map/reduce_scatter | solution.py:59
  463.9 258.8 %reduce-scatter.20.cloned.1.call-start = ((), (), s32[]{:S(2)}) async-start(), calls=%async_computation.27 | async-start | bytes 5242880 | tf_op jit(solution)/shard_map/reduce_scatter | solution.py:59
  516.7 34.1 %all-to-all-start.4 = ((bf16[4,128,1024]{2,1,0:T(8,128)(2,1)}), bf16[4,128,1024]{2,1,0:T(8,128)(2,1)S(1)}, u32[]{:S(2)}, u32[]{:S(2)}) async-start(bf16[4,128,1024]{2,1,0:T(8,128)(2,1)} %bitcast.167), calls=%async_computation.4 | async-start | bytes 2097152 | tf_op jit(solution)/shard_map/all_to_all | solution.py:63
  549.8 45.9 %copy-start.3 = (f32[128,1024]{1,0:T(8,128)S(1)}, f32[128,1024]{1,0:T(8,128)}, u32[]{:S(2)}) copy-start(f32[128,1024]{1,0:T(8,128)} %copy-done.2) | copy-start | bytes 1572868
  591.1 12.8 %all-to-all-start.5 = ((bf16[4,32,896]{2,1,0:T(8,128)(2,1)}), bf16[4,32,896]{2,1,0:T(8,128)(2,1)S(1)}, u32[]{:S(2)}, u32[]{:S(2)}) async-start(bf16[4,32,896]{2,1,0:T(8,128)(2,1)} %bitcast.182), calls=%async_computation.5 | async-start | bytes 458752 | tf_op jit(solution)/shard_map/all_to_all | solution.py:63
  648.2 77.4 %copy-start.5 = (bf16[256,2048]{1,0:T(8,128)(2,1)S(1)}, bf16[256,2048]{1,0:T(8,128)(2,1)}, u32[]{:S(2)}) copy-start(bf16[256,2048]{1,0:T(8,128)(2,1)} %reduce-scatter.18.cloned.1.call-done) | copy-start | bytes 3145732
  648.2 77.4 %collective-permute-start.3 = (bf16[128,2048]{1,0:T(8,128)(2,1)S(1)}, bf16[128,2048]{1,0:T(8,128)(2,1)S(1)}, u32[]{:S(2)}, u32[]{:S(2)}) collective-permute-start(bf16[128,2048]{1,0:T(8,128)(2,1)S(1)} %broadcast_select_fusion.4), channel_id=1, source_target_pairs={{0,4},{4,0},{1,5},{5,1},{2,6},{6,2},{3,7},{7,3},{8,12},{12,8},{9,1... | collective-permute-start | bytes 1572872 | tf_op jit(solution)/shard_map/ppermute | solution.py:67
  (34 other events, 79.0 us)
Sparse Core Ops, SparseCore 0:
  9.6 38.4 all-gather.10
  50.5 26.1 all-gather.12
  78.8 29.0 all-gather.22
  110.7 55.9 all-gather.16
  168.7 26.7 all-gather.14
  197.8 52.1 all-gather.24
  251.8 52.6 all-gather.26
  307.0 27.8 all-gather.18
  336.8 27.8 all-gather.20
  418.9 39.3 reduce-scatter.9
  462.0 41.2 reduce-scatter.13
  506.4 41.1 reduce-scatter.15
  551.4 39.6 reduce-scatter.21
  594.2 52.6 reduce-scatter.17
  649.0 19.6 reduce-scatter.11
  671.8 50.9 reduce-scatter.19
